TPU v7x, 512 devices: a whole 4x8x8 slice. The times are simulated.
512 devices in a mesh: seq: 64 (over y, z_hi, x), head: 8 (over z_lo, core).
Axes of the slice: x: 4, y: 8, z: 8 (z_hi: 2, z_lo: 4; z = z_hi * 4 + z_lo), core: 2. Of those that a mesh axis runs over, the one named last changes fastest.
Arguments:
- q_proj: bfloat16 [49152, 5120], P('seq', 'head'), may hold values from -500 to 500
- k_proj: bfloat16 [49152, 5120], P('seq', 'head'), may hold values from -500 to 500
- v_proj: bfloat16 [49152, 5120], P('seq', 'head'), may hold values from -6 to 6
- q_gain: float32 [5120], P('head'), may hold values from 0.25 to 1.75
- k_gain: float32 [5120], P('head'), may hold values from 0.25 to 1.75
- window_tiles: int32 [40, 128, 3], P('head'), may hold values from -2 to 127, as said below
- window_count: int32 [40, 128], P('head'), may hold values from 1 to 3
Outputs:
- attended: bfloat16 [49152, 5120], P('seq', 'head')
Inputs may be any that keep to these rules, and one draw needn't show every extreme that they name: Entry 0 of window_tiles[h, t] is t; the other entries are distinct tiles t - o with 1 <= o <= 2; negative entries are never seen.
All inputs are finite; a program needn't handle non-finite values.
Results may differ from a plain program's by a relative error of at most 0.012.
Values may be sent and summed in bfloat16 or wider, within the bound.
A program may use at most 64 MiB of HBM per device.

v0:
```python
import jax
import jax.numpy as jnp
from jax import lax
from jax.sharding import PartitionSpec as P

D = 5120
HEAD_DIM = 128
TILE = 384
DEV_TILES = 2
SPAN = 2
WIN = 3


NORM_EPS = 1e-06


def from_behind(value, axis, steps):
    count = lax.axis_size(axis)
    initial, last = (max(0, -steps), min(count, count - steps))
    return lax.ppermute(value, axis, [(source, source + steps) for source in range(initial, last)])


def row_squares(values):
    wide = values.astype(jnp.float32)
    return jnp.sum(wide * wide, axis=1)


def apply_norm(values, row_total, gain_vec):
    wide = values.astype(jnp.float32)
    return (wide * lax.rsqrt(row_total[:, None] / D + NORM_EPS) * gain_vec[None, :]).astype(
        jnp.bfloat16
    )


def softmax_bf(scores, key_mask):
    scores = jnp.where(key_mask, scores, -jnp.inf)
    row_max = jnp.max(scores, axis=-1, keepdims=True)
    exp_scores = jnp.where(key_mask, jnp.exp(scores - row_max), 0.0)
    return (exp_scores / jnp.sum(exp_scores, axis=-1, keepdims=True)).astype(jnp.bfloat16)


def heads_major(values, heads_here):
    return values.reshape(values.shape[0], heads_here, HEAD_DIM).transpose(1, 0, 2)


def local_attention(q_rows, k_buffer, v_buffer, relative, active, heads_here):
    row_count = q_rows.shape[0]
    key_tiles = SPAN + DEV_TILES
    scale = HEAD_DIM ** (-0.5)
    q_heads = heads_major(q_rows, heads_here)
    k_heads = heads_major(k_buffer, heads_here)
    v_heads = heads_major(v_buffer, heads_here)

    def one_head(per_head):
        q_one, k_one, v_one, rel_one, act_one = per_head
        matches = (rel_one[..., None] == jnp.arange(key_tiles)[None, None, :]) & act_one[..., None]
        tile_mask = jnp.any(matches, axis=1)
        key_mask = jnp.broadcast_to(tile_mask[:, None, :, None], (DEV_TILES, TILE, key_tiles, TILE))
        key_mask = key_mask.reshape(row_count, key_tiles * TILE)
        scores = jnp.einsum("qd,kd->qk", q_one, k_one, preferred_element_type=jnp.float32) * scale
        weights_bf = softmax_bf(scores, key_mask)
        result = jnp.dot(weights_bf, v_one, preferred_element_type=jnp.float32)
        return result.astype(jnp.bfloat16)

    outputs = lax.map(one_head, (q_heads, k_heads, v_heads, relative, active))
    return outputs.transpose(1, 0, 2).reshape(row_count, heads_here * HEAD_DIM)


def per_device(q_proj, k_proj, v_proj, q_gain, k_gain, window_tiles, window_count):
    seq_at = lax.axis_index("seq")
    row_count, local_cols = q_proj.shape
    heads_here = local_cols // HEAD_DIM
    margin_rows = SPAN * TILE
    totals = lax.psum((row_squares(q_proj), row_squares(k_proj)), "head")
    q_normed = apply_norm(q_proj, totals[0], q_gain)
    k_normed = apply_norm(k_proj, totals[1], k_gain)
    tail_pair = (k_normed, v_proj)
    halo_pair = from_behind((tail_pair[0], tail_pair[1]), "seq", 1)
    k_buffer = jnp.concatenate([halo_pair[0], k_normed], axis=0)
    v_buffer = jnp.concatenate([halo_pair[1], v_proj], axis=0)
    first_tile = seq_at * DEV_TILES
    tiles = lax.dynamic_slice_in_dim(window_tiles, first_tile, DEV_TILES, 1)
    counts = lax.dynamic_slice_in_dim(window_count, first_tile, DEV_TILES, 1)
    relative = tiles - (first_tile - SPAN)
    active = (jnp.arange(WIN)[None, None, :] < counts[:, :, None]) & (tiles >= 0)
    return local_attention(q_normed, k_buffer, v_buffer, relative, active, heads_here)


def solution(mesh):
    return jax.shard_map(
        per_device,
        mesh=mesh,
        in_specs=(
            P("seq", "head"),
            P("seq", "head"),
            P("seq", "head"),
            P("head"),
            P("head"),
            P("head", None, None),
            P("head", None),
        ),
        out_specs=P("seq", "head"),
        check_vma=False,
    )
```

profile of v0, /device:TPU:56, one launch (start us, length us, event | category | flops | bytes accessed | tf_op | source)
XLA Modules:
  0.0 166.3 jit_solution(17074162469571342933)
XLA Ops:
  0.0 1.6 copy.21
  1.6 1.6 copy.22
  3.6 19.3 %all-reduce = (f32[768]{0:T(1024)S(1)}, f32[768]{0:T(1024)S(1)}) all-reduce(f32[768]{0:T(1024)S(1)} %get-tuple-element.75, f32[768]{0:T(1024)S(1)} %get-tuple-element.76), channel_id=1, replica_groups=mesh['seq'=64,'head'=8] {'head'}, use_global_device_ids=true, to_apply=%region_1.0 | all-reduce | flops 1536 | bytes 12288 | tf_op jit(solution)/shard_map/psum | solution.py:74
  23.2 3.4 %collective-permute-start = (bf16[768,640]{0,1:T(8,128)(2,1)S(1)}, bf16[768,640]{0,1:T(8,128)(2,1)}, u32[]{:S(2)}, u32[]{:S(2)}) collective-permute-start(bf16[768,640]{0,1:T(8,128)(2,1)S(1)} %fusion.25), channel_id=1, source_target_pairs={{0,8},{8,16},{16,24},{24,32},{32,40},{40,48},{48,56},{56,64},{64,7... | collective-permute-start | bytes 2949128 | tf_op jit(solution)/shard_map/ppermute | solution.py:20
  26.6 1.6 copy.23
  28.2 3.4 %collective-permute-start.1 = (bf16[768,640]{0,1:T(8,128)(2,1)S(1)}, bf16[768,640]{0,1:T(8,128)(2,1)}, u32[]{:S(2)}, u32[]{:S(2)}) collective-permute-start(bf16[768,640]{0,1:T(8,128)(2,1)S(1)} %copy.23), channel_id=1, source_target_pairs={{0,8},{8,16},{16,24},{24,32},{32,40},{40,48},{48,56},{56,64},{64,7... | collective-permute-start | bytes 2949128 | tf_op jit(solution)/shard_map/ppermute | solution.py:20
  32.0 1.2 fusion.22
  33.2 48.0 %collective-permute-done = bf16[768,640]{0,1:T(8,128)(2,1)} collective-permute-done((bf16[768,640]{0,1:T(8,128)(2,1)S(1)}, bf16[768,640]{0,1:T(8,128)(2,1)}, u32[]{:S(2)}, u32[]{:S(2)}) %collective-permute-start) | collective-permute-done | bytes 983072 | tf_op jit(solution)/shard_map/ppermute | solution.py:20
  81.3 2.6 %pad_maximum_fusion = bf16[1536,640]{0,1:T(8,128)(2,1)} fusion(bf16[768,640]{0,1:T(8,128)(2,1)S(1)} %fusion.25, bf16[768,640]{0,1:T(8,128)(2,1)} %collective-permute-done), kind=kLoop, calls=%fused_computation.37 | loop fusion | flops 3932160 | bytes 3932160 | tf_op jit(solution)/shard_map/concatenate | solution.py:79
  83.9 32.5 %collective-permute-done.1 = bf16[768,640]{0,1:T(8,128)(2,1)} collective-permute-done((bf16[768,640]{0,1:T(8,128)(2,1)S(1)}, bf16[768,640]{0,1:T(8,128)(2,1)}, u32[]{:S(2)}, u32[]{:S(2)}) %collective-permute-start.1) | collective-permute-done | bytes 983072 | tf_op jit(solution)/shard_map/ppermute | solution.py:20
  116.4 2.6 %pad_maximum_fusion.1 = bf16[1536,640]{0,1:T(8,128)(2,1)} fusion(bf16[768,640]{0,1:T(8,128)(2,1)S(1)} %copy.23, bf16[768,640]{0,1:T(8,128)(2,1)} %collective-permute-done.1), kind=kLoop, calls=%fused_computation.38 | loop fusion | flops 3932160 | bytes 3932160 | tf_op jit(solution)/shard_map/concatenate | solution.py:80
  119.0 45.1 %while.10 = (s32[]{:T(128)}, bf16[5,768,128]{1,2,0:T(8,128)(2,1)}, s32[5,2,3]{2,1,0:T(2,128)S(1)}, pred[5,2,3]{2,1,0:T(4,128)(4,1)S(1)}, bf16[5,768,128]{1,2,0:T...) while((s32[]{:T(128)}, bf16[5,768,128]{1,2,0:T(8,128)(2,1)}, ...), condition=%wide.region_8.9_spmd, body=%wide.region_4.8_spmd.sunk | while | flops 620591680 | bytes 23217352 | solution.py:65
  120.4 2.3 %fusion.35 = (f32[768]{0:T(1024)S(1)}, f32[768,1536]{1,0:T(8,128)S(1)}) fusion(pred[768,1536]{1,0:T(8,128)(4,1)S(1)} %bitcast.54, bf16[5,1536,128]{1,2,0:T(8,128)(2,1)} %get-tuple-element.145, s32[]{:T(128)} %get-tuple-element.132, bf16[5,768,128]{1,2,0:T(8,128)(2,1)} %get-tuple-element.144), kind=kOutput, calls=%fused_computation.3.clone.1 | convolution fusion | flops 305528064 | bytes 6492160 | tf_op jit(solution)/shard_map/while/body/eval_jaxpr/qd,kd->qk/dot_general | solution.py:60
  122.6 1.5 fusion.36
  124.1 3.0 %fusion.37 = bf16[1,768,128]{2,1,0:T(8,128)(2,1)S(1)} fusion(pred[768,1536]{1,0:T(8,128)(4,1)S(1)} %bitcast.56, f32[768,1536]{1,0:T(8,128)S(1)} %get-tuple-element.122, f32[768]{0:T(1024)S(1)} %fusion.36, f32[768]{0:T(1024)S(1)} %get-tuple-element.123, bf16[5,1536,128]{1,2,0:T(8,128)(2,1)} %get-tuple-element.146, s32[]{:T(128)} %get-tuple-element.132), kind=kOutput, calls=%fused_computation.7.clone.1 | convolution fusion | flops 309166080 | bytes 6494720 | tf_op jit(solution)/shard_map/while/body/eval_jaxpr/dot_general | solution.py:62
  127.3 0.7 constant_dynamic-update-slice_fusion.2
  129.4 2.2 %fusion.35 = (f32[768]{0:T(1024)S(1)}, f32[768,1536]{1,0:T(8,128)S(1)}) fusion(pred[768,1536]{1,0:T(8,128)(4,1)S(1)} %bitcast.54, bf16[5,1536,128]{1,2,0:T(8,128)(2,1)} %get-tuple-element.145, s32[]{:T(128)} %get-tuple-element.132, bf16[5,768,128]{1,2,0:T(8,128)(2,1)} %get-tuple-element.144), kind=kOutput, calls=%fused_computation.3.clone.1 | convolution fusion | flops 305528064 | bytes 6492160 | tf_op jit(solution)/shard_map/while/body/eval_jaxpr/qd,kd->qk/dot_general | solution.py:60
  131.7 1.5 fusion.36
  133.1 3.0 %fusion.37 = bf16[1,768,128]{2,1,0:T(8,128)(2,1)S(1)} fusion(pred[768,1536]{1,0:T(8,128)(4,1)S(1)} %bitcast.56, f32[768,1536]{1,0:T(8,128)S(1)} %get-tuple-element.122, f32[768]{0:T(1024)S(1)} %fusion.36, f32[768]{0:T(1024)S(1)} %get-tuple-element.123, bf16[5,1536,128]{1,2,0:T(8,128)(2,1)} %get-tuple-element.146, s32[]{:T(128)} %get-tuple-element.132), kind=kOutput, calls=%fused_computation.7.clone.1 | convolution fusion | flops 309166080 | bytes 6494720 | tf_op jit(solution)/shard_map/while/body/eval_jaxpr/dot_general | solution.py:62
  138.4 2.2 %fusion.35 = (f32[768]{0:T(1024)S(1)}, f32[768,1536]{1,0:T(8,128)S(1)}) fusion(pred[768,1536]{1,0:T(8,128)(4,1)S(1)} %bitcast.54, bf16[5,1536,128]{1,2,0:T(8,128)(2,1)} %get-tuple-element.145, s32[]{:T(128)} %get-tuple-element.132, bf16[5,768,128]{1,2,0:T(8,128)(2,1)} %get-tuple-element.144), kind=kOutput, calls=%fused_computation.3.clone.1 | convolution fusion | flops 305528064 | bytes 6492160 | tf_op jit(solution)/shard_map/while/body/eval_jaxpr/qd,kd->qk/dot_general | solution.py:60
  140.7 1.5 fusion.36
  142.2 3.0 %fusion.37 = bf16[1,768,128]{2,1,0:T(8,128)(2,1)S(1)} fusion(pred[768,1536]{1,0:T(8,128)(4,1)S(1)} %bitcast.56, f32[768,1536]{1,0:T(8,128)S(1)} %get-tuple-element.122, f32[768]{0:T(1024)S(1)} %fusion.36, f32[768]{0:T(1024)S(1)} %get-tuple-element.123, bf16[5,1536,128]{1,2,0:T(8,128)(2,1)} %get-tuple-element.146, s32[]{:T(128)} %get-tuple-element.132), kind=kOutput, calls=%fused_computation.7.clone.1 | convolution fusion | flops 309166080 | bytes 6494720 | tf_op jit(solution)/shard_map/while/body/eval_jaxpr/dot_general | solution.py:62
  145.4 0.7 constant_dynamic-update-slice_fusion.2
  147.4 2.2 %fusion.35 = (f32[768]{0:T(1024)S(1)}, f32[768,1536]{1,0:T(8,128)S(1)}) fusion(pred[768,1536]{1,0:T(8,128)(4,1)S(1)} %bitcast.54, bf16[5,1536,128]{1,2,0:T(8,128)(2,1)} %get-tuple-element.145, s32[]{:T(128)} %get-tuple-element.132, bf16[5,768,128]{1,2,0:T(8,128)(2,1)} %get-tuple-element.144), kind=kOutput, calls=%fused_computation.3.clone.1 | convolution fusion | flops 305528064 | bytes 6492160 | tf_op jit(solution)/shard_map/while/body/eval_jaxpr/qd,kd->qk/dot_general | solution.py:60
  149.7 1.5 fusion.36
  151.2 3.0 %fusion.37 = bf16[1,768,128]{2,1,0:T(8,128)(2,1)S(1)} fusion(pred[768,1536]{1,0:T(8,128)(4,1)S(1)} %bitcast.56, f32[768,1536]{1,0:T(8,128)S(1)} %get-tuple-element.122, f32[768]{0:T(1024)S(1)} %fusion.36, f32[768]{0:T(1024)S(1)} %get-tuple-element.123, bf16[5,1536,128]{1,2,0:T(8,128)(2,1)} %get-tuple-element.146, s32[]{:T(128)} %get-tuple-element.132), kind=kOutput, calls=%fused_computation.7.clone.1 | convolution fusion | flops 309166080 | bytes 6494720 | tf_op jit(solution)/shard_map/while/body/eval_jaxpr/dot_general | solution.py:62
  154.4 0.7 constant_dynamic-update-slice_fusion.2
  156.4 2.2 %fusion.35 = (f32[768]{0:T(1024)S(1)}, f32[768,1536]{1,0:T(8,128)S(1)}) fusion(pred[768,1536]{1,0:T(8,128)(4,1)S(1)} %bitcast.54, bf16[5,1536,128]{1,2,0:T(8,128)(2,1)} %get-tuple-element.145, s32[]{:T(128)} %get-tuple-element.132, bf16[5,768,128]{1,2,0:T(8,128)(2,1)} %get-tuple-element.144), kind=kOutput, calls=%fused_computation.3.clone.1 | convolution fusion | flops 305528064 | bytes 6492160 | tf_op jit(solution)/shard_map/while/body/eval_jaxpr/qd,kd->qk/dot_general | solution.py:60
  158.7 1.5 fusion.36
  160.2 3.0 %fusion.37 = bf16[1,768,128]{2,1,0:T(8,128)(2,1)S(1)} fusion(pred[768,1536]{1,0:T(8,128)(4,1)S(1)} %bitcast.56, f32[768,1536]{1,0:T(8,128)S(1)} %get-tuple-element.122, f32[768]{0:T(1024)S(1)} %fusion.36, f32[768]{0:T(1024)S(1)} %get-tuple-element.123, bf16[5,1536,128]{1,2,0:T(8,128)(2,1)} %get-tuple-element.146, s32[]{:T(128)} %get-tuple-element.132), kind=kOutput, calls=%fused_computation.7.clone.1 | convolution fusion | flops 309166080 | bytes 6494720 | tf_op jit(solution)/shard_map/while/body/eval_jaxpr/dot_general | solution.py:62
  163.4 0.7 constant_dynamic-update-slice_fusion.2
  164.1 2.2 %copy.29 = bf16[768,640]{1,0:T(8,128)(2,1)} copy(bf16[768,640]{0,1:T(8,128)(2,1)} %bitcast.58) | data formatting | bytes 1966080 | tf_op jit(solution)/shard_map/reshape | solution.py:66
  (49 shorter events, 9.3 us)
Async XLA Ops:
  0.0 31.6 %copy-start = (s32[5,128,3]{1,2,0:T(4,128)S(1)}, s32[5,128,3]{1,2,0:T(4,128)}, u32[]{:S(2)}) copy-start(s32[5,128,3]{1,2,0:T(4,128)} %param.14) | copy-start | bytes 23044
  0.0 22.9 %copy-start.1 = (f32[640]{0:T(1024)S(1)}, f32[640]{0:T(1024)}, u32[]{:S(2)}) copy-start(f32[640]{0:T(1024)} %param.13) | copy-start | bytes 7684
  1.6 30.1 %copy-start.3 = (s32[5,128]{1,0:T(8,128)S(1)}, s32[5,128]{1,0:T(8,128)}, u32[]{:S(2)}) copy-start(s32[5,128]{1,0:T(8,128)} %param.15) | copy-start | bytes 7684
  1.6 30.4 %copy-start.2 = (f32[640]{0:T(1024)S(1)}, f32[640]{0:T(1024)}, u32[]{:S(2)}) copy-start(f32[640]{0:T(1024)} %param.12) | copy-start | bytes 7684
  23.2 58.0 %collective-permute-start = (bf16[768,640]{0,1:T(8,128)(2,1)S(1)}, bf16[768,640]{0,1:T(8,128)(2,1)}, u32[]{:S(2)}, u32[]{:S(2)}) collective-permute-start(bf16[768,640]{0,1:T(8,128)(2,1)S(1)} %fusion.25), channel_id=1, source_target_pairs={{0,8},{8,16},{16,24},{24,32},{32,40},{40,48},{48,56},{56,64},{64,7... | collective-permute-start | bytes 2949128 | tf_op jit(solution)/shard_map/ppermute | solution.py:20
  28.2 88.2 %collective-permute-start.1 = (bf16[768,640]{0,1:T(8,128)(2,1)S(1)}, bf16[768,640]{0,1:T(8,128)(2,1)}, u32[]{:S(2)}, u32[]{:S(2)}) collective-permute-start(bf16[768,640]{0,1:T(8,128)(2,1)S(1)} %copy.23), channel_id=1, source_target_pairs={{0,8},{8,16},{16,24},{24,32},{32,40},{40,48},{48,56},{56,64},{64,7... | collective-permute-start | bytes 2949128 | tf_op jit(solution)/shard_map/ppermute | solution.py:20
where the time goes:
time: 167 us; the launch traced here: 166 us
  waiting for transfers between devices  80.5 us (48%)
  matrix products  26.5 us (16%)
  blocking collectives  19.3 us (12%)
  local copies, waits for them, and re-layouts  17.9 us (11%)
  other arithmetic  15.2 us (9%)
  starting transfers between devices  6.8 us (4%)
    ppermute x2, waiting for transfers between devices, from_behind(): lax.ppermute(value, axis, [(source, source + steps) for source in range(i...  80.5 us
    psum x1, blocking collectives, per_device(): totals = lax.psum((row_squares(q_proj), row_squares(k_proj)), 'head')  19.3 us
    dot_general x5, matrix products, one_head(): result = jnp.dot(weights_bf, v_one, preferred_element_type=jnp.float32)  15.2 us
    dot_general x5, matrix products, one_head(): jnp.einsum('qd,kd->qk', q_one, k_one, preferred_element_type=jnp.float32)  11.2 us
    reduce_sum x5, other arithmetic, softmax_bf(): jnp.sum(exp_scores, axis=-1, keepdims=True)  7.43 us
    ppermute x2, starting transfers between devices, from_behind(): lax.ppermute(value, axis, [(source, source + steps) for source in range(i...  6.8 us
    unnamed x12, local copies, waits for them, and re-layouts  4.9 us
    dynamic_update_slice x10, local copies, waits for them, and re-layouts, local_attention(): outputs = lax.map(one_head, (q_heads, k_heads, v_heads, relative, active))  4.19 us
  transfers between devices with their start and end apart: 2, of which 2 were waited for; matrix products, arithmetic and copies ran while one was open for 3% of the time, Pallas kernels for 0%

commit v1 on v0

v1 whole, which is shorter than its diff:
```python
import functools
import math

import jax
import jax.numpy as jnp
from jax import lax
from jax.experimental import pallas as pl
from jax.experimental.pallas import tpu as pltpu
from jax.sharding import PartitionSpec as P

HEAD_DIM = 128
WIN = 3
NORM_EPS = 1e-06
EXP_SCALE = math.log2(math.e) / math.sqrt(HEAD_DIM)
LOW = -1e30
HIGH = 1e30
F32 = jnp.float32
BF16 = jnp.bfloat16
MESH = pl.DeviceIdType.MESH


def dot_nt(a, b):
    return lax.dot_general(a, b, (((1,), (1,)), ((), ())), preferred_element_type=F32)


def dot_tn(a, b):
    return lax.dot_general(a, b, (((0,), (0,)), ((), ())), preferred_element_type=F32)


def routes(heads):
    units = 4 * heads
    via_two = [u for u in range(units - 2) if u % 3 == 0][: (units * 3) // 10]
    via_zero = [u for u in range(units) if u % 3 == 1]
    direct = [u for u in range(units) if u not in via_two and u not in via_zero]
    return via_two, via_zero, direct


def kernel(
    seqs,
    group,
    q_hbm,
    k_hbm,
    v_hbm,
    qg_ref,
    kg_ref,
    tiles_ref,
    count_ref,
    out_hbm,
    ql,
    kl,
    vl,
    halo,
    relay_buf,
    q_next,
    o_send,
    o_recv,
    ml_send,
    ml_recv,
    acc,
    ml,
    col_own,
    col_prev,
    col_next,
    stats,
    inv_own,
    inv_prev,
    inv_next,
    out_buf,
    load_sem,
    unit_send,
    unit_recv,
    relay_send,
    relay_recv,
    q_send_sem,
    q_recv_sem,
    o_send_sem,
    o_recv_sem,
    ml_sem,
    stat_send,
    stat_recv,
    inv_sem,
    out_sem,
):
    heads, rows, _ = ql.shape
    tile = rows // 2
    model = heads * HEAD_DIM * group
    units = 4 * heads
    via_two, via_zero, direct = routes(heads)
    s = lax.axis_index("seq")
    me = lax.axis_index("head")
    x = lax.rem(s, 4)
    first = s * 2

    def at(step):
        return {"seq": lax.rem(s + step + seqs, seqs), "head": me}

    def remote(src, dst, send, recv, where):
        return pltpu.make_async_remote_copy(
            src_ref=src, dst_ref=dst, send_sem=send, recv_sem=recv, device_id=where, device_id_type=MESH
        )

    def loads(which):
        src, dst = ((q_hbm, ql), (k_hbm, kl), (v_hbm, vl))[which]
        return [
            pltpu.make_async_copy(src.at[:, pl.ds(h * HEAD_DIM, HEAD_DIM)], dst.at[h], load_sem.at[which, h])
            for h in range(heads)
        ]

    for which in range(3):
        for copy in loads(which):
            copy.start()

    barrier = pltpu.get_barrier_semaphore()

    def greet(where):
        pl.semaphore_signal(barrier, inc=1, device_id=where, device_id_type=MESH)

    greet(at(1))
    greet(at(-1))

    @pl.when((x == 0) | (x == 2))
    def _():
        greet(at(3))

    @pl.when((x == 1) | (x == 3))
    def _():
        greet(at(-3))

    @pl.when(x == 0)
    def _():
        greet(at(4))
        greet(at(-4))

    for d in range(1, group):
        greet({"seq": s, "head": lax.rem(me + d, group)})

    ones = jnp.ones((8, HEAD_DIM), BF16)
    for which, buf in ((0, ql), (1, kl)):
        for copy in loads(which):
            copy.wait()

        def square_sum(h, total, buf=buf):
            wide = buf[h].astype(F32)
            sq = wide * wide
            hi = sq.astype(BF16)
            lo = (sq - hi.astype(F32)).astype(BF16)
            return total + dot_nt(ones, hi) + dot_nt(ones, lo)

        total = lax.fori_loop(0, heads, square_sum, jnp.zeros((8, rows), F32))
        stats[me, :, which * rows : (which + 1) * rows] = total[:1]

    @pl.when(x == 0)
    def _():
        pl.semaphore_wait(barrier, group - 1 + 5)

    @pl.when(x > 0)
    def _():
        pl.semaphore_wait(barrier, group - 1 + 3)

    def stat_copy(d):
        return remote(
            stats.at[me], stats.at[me], stat_send.at[d], stat_recv.at[me], {"seq": s, "head": lax.rem(me + d, group)}
        )

    for d in range(1, group):
        stat_copy(d).start()

    def unit_src(u):
        h, part = u // 4, u % 4
        src = v_hbm if part % 2 else k_hbm
        row = 0 if part >= 2 else tile
        return src.at[pl.ds(row, tile), pl.ds(h * HEAD_DIM, HEAD_DIM)]

    def near_copy(u):
        return remote(unit_src(u), halo.at[u], unit_send.at[u], unit_recv.at[u], at(1))

    def far_copy(u):
        if u in via_two:
            i = via_two.index(u)
            return remote(unit_src(u), relay_buf.at[i], unit_send.at[u], relay_recv.at[i], at(-1))
        if u in via_zero:
            i = via_zero.index(u)
            return remote(unit_src(u), relay_buf.at[i], unit_send.at[u], relay_recv.at[i], at(-3))
        return remote(unit_src(u), halo.at[u], unit_send.at[u], unit_recv.at[u], at(1))

    near_units = [u for u in range(units) if u % 4 < 2]

    def q_copy(h):
        return remote(
            q_hbm.at[pl.ds(0, tile), pl.ds(h * HEAD_DIM, HEAD_DIM)],
            q_next.at[h],
            q_send_sem.at[h],
            q_recv_sem.at[h],
            at(-1),
        )

    @pl.when(x == 3)
    def _():
        for u in range(units):
            far_copy(u).start()

    @pl.when(x < 3)
    def _():
        for u in near_units:
            near_copy(u).start()

    @pl.when(x > 0)
    def _():
        for h in range(heads):
            q_copy(h).start()

    def relay_copy(i, at_x):
        if at_x == 0:
            u = via_zero[i]
            return remote(relay_buf.at[i], halo.at[u], relay_send.at[i], unit_recv.at[u], at(4))
        if at_x == 1:
            u = via_two[i]
            return remote(relay_buf.at[i], halo.at[u], relay_send.at[i], unit_recv.at[u], at(-1))
        return remote(relay_buf.at[i], relay_buf.at[i], relay_send.at[i], relay_recv.at[i], at(3))

    def relay_count(at_x):
        return len(via_zero) if at_x == 0 else len(via_two)

    def relay(i, places):
        for at_x in places:
            if i < relay_count(at_x):

                @pl.when(x == at_x)
                def _(at_x=at_x):
                    copy = remote(relay_buf.at[i], relay_buf.at[i], relay_send.at[i], relay_recv.at[i], at(3))
                    copy.wait_recv()
                    relay_copy(i, at_x).start()

    for d in range(1, group):
        other = lax.rem(me + group - d, group)
        remote(stats.at[other], stats.at[other], stat_send.at[d], stat_recv.at[other], at(1)).wait_recv()
    inv_own[...] = lax.rsqrt(jnp.sum(stats[...], axis=0) / model + NORM_EPS)

    def inv_copy(side):
        dst = (inv_prev, inv_next)[side]
        return remote(inv_own, dst, inv_sem.at[side], inv_sem.at[2 + side], at((1, -1)[side]))

    inv_copy(0).start()

    @pl.when(x > 0)
    def _():
        inv_copy(1).start()

    def to_columns(row):
        return jnp.transpose(jnp.broadcast_to(row, (HEAD_DIM, row.shape[1])))

    def normed(values, column, gain):
        return (values.astype(F32) * column * gain).astype(BF16)

    def gain_row(ref, h):
        return ref[h]

    col_own[...] = to_columns(inv_own[...])

    def norm_own(h, carry):
        ql[h] = normed(ql[h], col_own[:rows], gain_row(qg_ref, h))
        kl[h] = normed(kl[h], col_own[rows:], gain_row(kg_ref, h))
        return carry

    lax.fori_loop(0, heads, norm_own, 0)
    for copy in loads(2):
        copy.wait()

    def seen(h, t, back):
        target = t - back
        count = count_ref[h, t]
        hit = jnp.int32(0)
        for w in range(WIN):
            hit = hit + jnp.where((tiles_ref[h, w, t] == target) & (w < count), 1, 0)
        return jnp.where((hit > 0) & (target >= 0), 1.0, 0.0).astype(F32)

    def top(scores, flag):
        return jnp.max(scores, axis=0, keepdims=True) * flag + (1.0 - flag) * LOW

    def shift(peak, flag):
        return peak * flag + (1.0 - flag) * HIGH

    def exps(scores, shifted):
        return jnp.exp2((scores - shifted) * EXP_SCALE)

    def row_sum(values):
        return jnp.sum(values, axis=0, keepdims=True)

    def two_blocks(keys, values, queries, flag_lo, flag_hi):
        scores = dot_nt(keys, queries)
        s_lo, s_hi = scores[:tile], scores[tile:]
        m_lo = top(s_lo, flag_lo)
        m_hi = jnp.max(s_hi, axis=0, keepdims=True) if flag_hi is None else top(s_hi, flag_hi)
        peak = jnp.maximum(m_lo, m_hi)
        p_lo = exps(s_lo, shift(peak, flag_lo))
        p_hi = exps(s_hi, peak if flag_hi is None else shift(peak, flag_hi))
        total = row_sum(p_lo) + row_sum(p_hi)
        mixed = dot_tn(values[:tile], p_lo.astype(BF16)) + dot_tn(values[tile:], p_hi.astype(BF16))
        return peak, total, mixed

    def local(h, carry):
        keys, values = kl[h], vl[h]
        scores = dot_nt(keys[:tile], ql[h, :tile])
        peak = jnp.max(scores, axis=0, keepdims=True)
        probs = exps(scores, peak)
        ml[h, 0:1] = peak
        ml[h, 1:2] = row_sum(probs)
        acc[h, 0] = dot_tn(values[:tile], probs.astype(BF16))
        peak, total, mixed = two_blocks(keys, values, ql[h, tile:], seen(h, first + 1, 1), None)
        ml[h, 2:3] = peak
        ml[h, 3:4] = total
        acc[h, 1] = mixed
        return carry

    def o_copy(h):
        return remote(o_send.at[h], o_recv.at[h], o_send_sem.at[h], o_recv_sem.at[h], at(1))

    def ml_copy():
        return remote(ml_send, ml_recv, ml_sem.at[0], ml_sem.at[1], at(1))

    def for_next(h, carry):
        q_copy(h).wait_recv()
        queries = normed(q_next[h], col_next[...], gain_row(qg_ref, h))
        peak, total, mixed = two_blocks(
            kl[h], vl[h], queries, seen(h, first + 2, 2), seen(h, first + 2, 1)
        )
        ml_send[h, 0:1] = peak
        ml_send[h, 1:2] = total
        o_send[h] = mixed.astype(BF16)
        o_copy(h).start()
        return carry

    relay(0, (0, 2))
    lax.fori_loop(0, heads, local, 0)
    relay(1, (0, 2))

    @pl.when(x < 3)
    def _():
        inv_copy(1).wait_recv()
        col_next[...] = to_columns(inv_next[:, :tile])
        lax.fori_loop(0, heads, for_next, 0)
        ml_copy().start()

    inv_copy(0).wait_recv()
    col_prev[...] = to_columns(inv_prev[:, rows:])

    def finish(h, part, total, mixed):
        out_buf[h, part * tile : (part + 1) * tile] = jnp.transpose(mixed * (1.0 / total)).astype(BF16)

    def out_copy(h):
        return pltpu.make_async_copy(
            out_buf.at[h], out_hbm.at[:, pl.ds(pl.multiple_of(h * HEAD_DIM, HEAD_DIM), HEAD_DIM)], out_sem.at[h]
        )

    def unit_wait(u):
        remote(halo.at[u], halo.at[u], unit_send.at[u], unit_recv.at[u], at(1)).wait_recv()

    def high_tile(h):
        keys = normed(halo[4 * h], col_prev[tile:], gain_row(kg_ref, h))
        values = halo[4 * h + 1]
        flag = seen(h, first + 1, 2)
        scores = dot_nt(keys, ql[h, tile:])
        before = ml[h, 2:3]
        peak = jnp.maximum(before, top(scores, flag))
        probs = exps(scores, shift(peak, flag))
        fade = exps(before, peak)
        total = ml[h, 3:4] * fade + row_sum(probs)
        mixed = acc[h, 1] * fade + dot_tn(values, probs.astype(BF16))
        finish(h, 1, total, mixed)
        return keys

    def far_head(h):
        for part in range(4):
            unit_wait(4 * h + part)
        keys_hi = high_tile(h)
        keys_lo = normed(halo[4 * h + 2], col_prev[:tile], gain_row(kg_ref, h))
        keys = jnp.concatenate([keys_lo, keys_hi], axis=0)
        values = jnp.concatenate([halo[4 * h + 3], halo[4 * h + 1]], axis=0)
        peak_far, total_far, mixed_far = two_blocks(
            keys, values, ql[h, :tile], seen(h, first, 2), seen(h, first, 1)
        )
        merge(h, peak_far, total_far, mixed_far)

    def merge(h, peak_far, total_far, mixed_far):
        before = ml[h, 0:1]
        peak = jnp.maximum(before, peak_far)
        fade, fade_far = exps(before, peak), exps(peak_far, peak)
        finish(h, 0, ml[h, 1:2] * fade + total_far * fade_far, acc[h, 0] * fade + mixed_far * fade_far)
        out_copy(h).start()

    def near_high(h, carry):
        unit_wait(4 * h)
        unit_wait(4 * h + 1)
        high_tile(h)
        return carry

    def near_low(h, carry):
        o_copy(h).wait_recv()
        merge(h, ml_recv[h, 0:1], ml_recv[h, 1:2], o_recv[h].astype(F32))
        return carry

    def loop(lo, hi, body):
        lax.fori_loop(lo, hi, lambda h, c: body(h, c), 0)

    @pl.when(x == 0)
    def _():
        done = 2
        for h in range(heads):
            need = (4 * h + 2) // 3 + 2
            while done < min(need, len(via_zero)):
                relay(done, (0,))
                done += 1
            far_head(h)
        while done < len(via_zero):
            relay(done, (0,))
            done += 1

    for at_x, start in ((1, 0), (2, 2)):

        @pl.when(x == at_x)
        def _(at_x=at_x, start=start):
            left = list(range(start, len(via_two)))
            split = max(0, len(left) - heads)
            for i in left[:split]:
                relay(i, (at_x,))
            left = left[split:]
            for h in range(heads):
                if h < len(left):
                    relay(left[h], (at_x,))
                near_high(h, 0)

    @pl.when(x == 3)
    def _():
        loop(0, heads, near_high)

    @pl.when(x > 0)
    def _():
        ml_copy().wait_recv()
        loop(0, heads, near_low)

    for h in range(heads):
        out_copy(h).wait()
    for d in range(1, group):
        stat_copy(d).wait_send()
    inv_copy(0).wait_send()

    @pl.when(x > 0)
    def _():
        inv_copy(1).wait_send()
        for h in range(heads):
            q_copy(h).wait_send()

    @pl.when(x == 3)
    def _():
        for u in range(units):
            far_copy(u).wait_send()

    @pl.when(x < 3)
    def _():
        for u in near_units:
            near_copy(u).wait_send()
        for h in range(heads):
            o_copy(h).wait_send()
        ml_copy().wait_send()

    for at_x in range(3):

        @pl.when(x == at_x)
        def _(at_x=at_x):
            for i in range(relay_count(at_x)):
                relay_copy(i, at_x).wait_send()


def per_device(q_proj, k_proj, v_proj, q_gain, k_gain, window_tiles, window_count):
    seqs, group = lax.axis_size("seq"), lax.axis_size("head")
    rows, cols = q_proj.shape
    heads, tile = cols // HEAD_DIM, rows // 2
    units = 4 * heads
    via_two, via_zero, _ = routes(heads)
    slots = max(len(via_two), len(via_zero))
    dma = pltpu.SemaphoreType.DMA
    anywhere = pl.BlockSpec(memory_space=pl.ANY)
    vmem = pl.BlockSpec(memory_space=pltpu.VMEM)
    smem = pl.BlockSpec(memory_space=pltpu.SMEM)
    flops = 30 * heads * tile * tile * HEAD_DIM
    return pl.pallas_call(
        functools.partial(kernel, seqs, group),
        out_shape=jax.ShapeDtypeStruct((rows, cols), BF16),
        in_specs=[anywhere] * 3 + [vmem] * 2 + [smem] * 2,
        out_specs=anywhere,
        scratch_shapes=[
            pltpu.VMEM((heads, rows, HEAD_DIM), BF16),
            pltpu.VMEM((heads, rows, HEAD_DIM), BF16),
            pltpu.VMEM((heads, rows, HEAD_DIM), BF16),
            pltpu.VMEM((units, tile, HEAD_DIM), BF16),
            pltpu.VMEM((slots, tile, HEAD_DIM), BF16),
            pltpu.VMEM((heads, tile, HEAD_DIM), BF16),
            pltpu.VMEM((heads, HEAD_DIM, tile), BF16),
            pltpu.VMEM((heads, HEAD_DIM, tile), BF16),
            pltpu.VMEM((heads, 2, tile), F32),
            pltpu.VMEM((heads, 2, tile), F32),
            pltpu.VMEM((heads, 2, HEAD_DIM, tile), F32),
            pltpu.VMEM((heads, 4, tile), F32),
            pltpu.VMEM((2 * rows, HEAD_DIM), F32),
            pltpu.VMEM((rows, HEAD_DIM), F32),
            pltpu.VMEM((tile, HEAD_DIM), F32),
            pltpu.VMEM((group, 1, 2 * rows), F32),
            pltpu.VMEM((1, 2 * rows), F32),
            pltpu.VMEM((1, 2 * rows), F32),
            pltpu.VMEM((1, 2 * rows), F32),
            pltpu.VMEM((heads, rows, HEAD_DIM), BF16),
            dma((3, heads)),
            dma((units,)),
            dma((units,)),
            dma((slots,)),
            dma((slots,)),
            dma((heads,)),
            dma((heads,)),
            dma((heads,)),
            dma((heads,)),
            dma((2,)),
            dma((group,)),
            dma((group,)),
            dma((4,)),
            dma((heads,)),
        ],
        compiler_params=pltpu.CompilerParams(
            collective_id=0, has_side_effects=True, vmem_limit_bytes=48 * 1024 * 1024
        ),
        cost_estimate=pl.CostEstimate(flops=flops, bytes_accessed=4 * rows * cols * 2, transcendentals=0),
        name="window_attention",
    )(
        q_proj,
        k_proj,
        v_proj,
        q_gain.reshape(heads, 1, HEAD_DIM),
        k_gain.reshape(heads, 1, HEAD_DIM),
        window_tiles.transpose(0, 2, 1),
        window_count,
    )


def solution(mesh):
    return jax.shard_map(
        per_device,
        mesh=mesh,
        in_specs=(
            P("seq", "head"),
            P("seq", "head"),
            P("seq", "head"),
            P("head"),
            P("head"),
            P("head", None, None),
            P("head", None),
        ),
        out_specs=P("seq", "head"),
        check_vma=False,
    )
```

time: 167 us -> 94.2 us (0.56)
  the two profiles are of different devices: /device:TPU:56 before, /device:TPU:48 now
where the time goes in v1:
time: 94.2 us; the launch traced here: 93.9 us
  Pallas kernels  87.9 us (93%)
  local copies, waits for them, and re-layouts  5.97 us (6%)
    pallas_call x1, Pallas kernels, per_device(): pl.pallas_call(functools.partial(kernel, seqs, group), out_shape=jax.Shap...  87.9 us
    unnamed x11, local copies, waits for them, and re-layouts  4.56 us

profile of v1, /device:TPU:48, one launch (start us, length us, event | category | flops | bytes accessed | tf_op | source)
XLA Modules:
  0.0 93.9 jit_solution(902877823545920885)
XLA Ops:
  0.0 0.0 copy-start.3
  0.0 0.7 reshape.6.qg_ref
  0.7 0.0 copy-start.4
  0.7 0.7 reshape.7.kg_ref
  1.4 0.0 copy-done.3
  1.4 0.0 copy-done.4
  1.4 0.0 copy-start
  1.4 1.2 %copy-done = bf16[768,640]{1,0:T(8,128)(2,1)S(1)} copy-done((bf16[768,640]{1,0:T(8,128)(2,1)S(1)}, bf16[768,640]{1,0:T(8,128)(2,1)}, u32[]{:S(2)}) %copy-start) | copy-done | bytes 983064
  2.6 0.0 copy-start.1
  2.6 1.2 %copy-done.1 = bf16[768,640]{1,0:T(8,128)(2,1)S(1)} copy-done((bf16[768,640]{1,0:T(8,128)(2,1)S(1)}, bf16[768,640]{1,0:T(8,128)(2,1)}, u32[]{:S(2)}) %copy-start.1) | copy-done | bytes 983064
  3.8 0.0 copy-start.2
  3.8 1.2 %copy-done.2 = bf16[768,640]{1,0:T(8,128)(2,1)S(1)} copy-done((bf16[768,640]{1,0:T(8,128)(2,1)S(1)}, bf16[768,640]{1,0:T(8,128)(2,1)}, u32[]{:S(2)}) %copy-start.2) | copy-done | bytes 983064
  5.0 87.9 %window_attention.1 = bf16[768,640]{1,0:T(8,128)(2,1)S(1)} custom-call(bf16[768,640]{1,0:T(8,128)(2,1)S(1)} %copy-done, bf16[768,640]{1,0:T(8,128)(2,1)S(1)} %copy-done.1, bf16[768,640]{1,0:T(8,128)(2,1)S(1)} %copy-done.2, f32[5,1,128]{2,1,0:T(1,128)S(1)} %reshape.6.qg_ref, f32[5,1,128]{2,1,0:T(1,128)S(1)} %reshape.7.kg_ref, s32[5,3,128]{2,1,0:T(4,128)S(1)} %bitcast.1, ...), custom_call_target="tpu_custom_call" | custom-call | flops 2831155200 | bytes 3932160 | tf_op jit(solution)/shard_map/window_attention/pallas_call | solution.py:486
  93.0 0.9 %copy.9 = bf16[768,640]{1,0:T(8,128)(2,1)} copy(bf16[768,640]{1,0:T(8,128)(2,1)S(1)} %window_attention.1) | data formatting | bytes 1966080
Async XLA Ops:
  0.0 1.4 %copy-start.3 = (s32[5,128,3]{1,2,0:T(4,128)S(1)}, s32[5,128,3]{1,2,0:T(4,128)}, u32[]{:S(2)}) copy-start(s32[5,128,3]{1,2,0:T(4,128)} %param.12) | copy-start | bytes 23044
  0.7 0.7 copy-start.4
  1.4 1.2 %copy-start = (bf16[768,640]{1,0:T(8,128)(2,1)S(1)}, bf16[768,640]{1,0:T(8,128)(2,1)}, u32[]{:S(2)}) copy-start(bf16[768,640]{1,0:T(8,128)(2,1)} %q_hbm.1) | copy-start | bytes 2949124
  2.6 1.2 %copy-start.1 = (bf16[768,640]{1,0:T(8,128)(2,1)S(1)}, bf16[768,640]{1,0:T(8,128)(2,1)}, u32[]{:S(2)}) copy-start(bf16[768,640]{1,0:T(8,128)(2,1)} %k_hbm.1) | copy-start | bytes 2949124
  3.8 1.2 %copy-start.2 = (bf16[768,640]{1,0:T(8,128)(2,1)S(1)}, bf16[768,640]{1,0:T(8,128)(2,1)}, u32[]{:S(2)}) copy-start(bf16[768,640]{1,0:T(8,128)(2,1)} %v_hbm.1) | copy-start | bytes 2949124

commit v2 on v1

--- a/solution.py
+++ b/solution.py
@@ -27,11 +27,17 @@
     return lax.dot_general(a, b, (((0,), (0,)), ((), ())), preferred_element_type=F32)
 
 
+SUB = 2
+FAR_EARLY = 3
+NEAR_EARLY = 2
+
+
 def routes(heads):
-    units = 4 * heads
-    via_two = [u for u in range(units - 2) if u % 3 == 0][: (units * 3) // 10]
-    via_zero = [u for u in range(units) if u % 3 == 1]
-    direct = [u for u in range(units) if u not in via_two and u not in via_zero]
+    chunks = 4 * heads * SUB
+    two, zero = (chunks * 3) // 10, (chunks * 13) // 40
+    via_two = [3 * i for i in range(two)]
+    via_zero = [3 * i + 1 for i in range(zero)]
+    direct = [c for c in range(chunks) if c not in via_two and c not in via_zero]
     return via_two, via_zero, direct
 
 
@@ -49,6 +55,8 @@
     ql,
     kl,
     vl,
+    qn,
+    kn,
     halo,
     relay_buf,
     q_next,
@@ -84,7 +92,8 @@
     heads, rows, _ = ql.shape
     tile = rows // 2
     model = heads * HEAD_DIM * group
-    units = 4 * heads
+    piece = tile // SUB
+    chunks = 4 * heads * SUB
     via_two, via_zero, direct = routes(heads)
     s = lax.axis_index("seq")
     me = lax.axis_index("head")
@@ -149,6 +158,9 @@
         total = lax.fori_loop(0, heads, square_sum, jnp.zeros((8, rows), F32))
         stats[me, :, which * rows : (which + 1) * rows] = total[:1]
 
+    for copy in loads(2):
+        copy.wait()
+
     @pl.when(x == 0)
     def _():
         pl.semaphore_wait(barrier, group - 1 + 5)
@@ -165,57 +177,64 @@
     for d in range(1, group):
         stat_copy(d).start()
 
-    def unit_src(u):
-        h, part = u // 4, u % 4
-        src = v_hbm if part % 2 else k_hbm
-        row = 0 if part >= 2 else tile
-        return src.at[pl.ds(row, tile), pl.ds(h * HEAD_DIM, HEAD_DIM)]
-
-    def near_copy(u):
-        return remote(unit_src(u), halo.at[u], unit_send.at[u], unit_recv.at[u], at(1))
-
-    def far_copy(u):
-        if u in via_two:
-            i = via_two.index(u)
-            return remote(unit_src(u), relay_buf.at[i], unit_send.at[u], relay_recv.at[i], at(-1))
-        if u in via_zero:
-            i = via_zero.index(u)
-            return remote(unit_src(u), relay_buf.at[i], unit_send.at[u], relay_recv.at[i], at(-3))
-        return remote(unit_src(u), halo.at[u], unit_send.at[u], unit_recv.at[u], at(1))
-
-    near_units = [u for u in range(units) if u % 4 < 2]
+    def chunk_src(c):
+        h, part, sub = c // (4 * SUB), (c // SUB) % 4, c % SUB
+        src = vl if part % 2 else kl
+        return src.at[h, pl.ds((0 if part >= 2 else tile) + sub * piece, piece)]
+
+    def near_copies(h):
+        return [
+            remote(
+                src.at[h, pl.ds(tile + sub * piece, piece)],
+                halo.at[4 * SUB * h + part * SUB + sub],
+                unit_send.at[4 * SUB * h + part * SUB + sub],
+                unit_recv.at[4 * SUB * h + part * SUB + sub],
+                at(1),
+            )
+            for part, src in ((0, kl), (1, vl))
+            for sub in range(SUB)
+        ]
+
+    def far_copy(c):
+        if c in via_two:
+            i = via_two.index(c)
+            return remote(chunk_src(c), relay_buf.at[i], unit_send.at[c], relay_recv.at[i], at(-1))
+        if c in via_zero:
+            i = via_zero.index(c)
+            return remote(chunk_src(c), relay_buf.at[i], unit_send.at[c], relay_recv.at[i], at(-3))
+        return remote(chunk_src(c), halo.at[c], unit_send.at[c], unit_recv.at[c], at(1))
 
     def q_copy(h):
-        return remote(
-            q_hbm.at[pl.ds(0, tile), pl.ds(h * HEAD_DIM, HEAD_DIM)],
-            q_next.at[h],
-            q_send_sem.at[h],
-            q_recv_sem.at[h],
-            at(-1),
-        )
+        return remote(ql.at[h, pl.ds(0, tile)], q_next.at[h], q_send_sem.at[h], q_recv_sem.at[h], at(-1))
+
+    early = min(FAR_EARLY, chunks)
+    near_early = min(NEAR_EARLY, heads)
 
     @pl.when(x == 3)
     def _():
-        for u in range(units):
-            far_copy(u).start()
-
-    @pl.when(x < 3)
-    def _():
-        for u in near_units:
-            near_copy(u).start()
-
-    @pl.when(x > 0)
+        for c in range(early):
+            far_copy(c).start()
+            if c % 2 == 1 and c // 2 < heads:
+                q_copy(c // 2).start()
+        for h in range(early // 2, heads):
+            q_copy(h).start()
+
+    @pl.when((x > 0) & (x < 3))
     def _():
         for h in range(heads):
             q_copy(h).start()
 
+    @pl.when(x < 3)
+    def _():
+        for h in range(near_early):
+            for copy in near_copies(h):
+                copy.start()
+
     def relay_copy(i, at_x):
         if at_x == 0:
-            u = via_zero[i]
-            return remote(relay_buf.at[i], halo.at[u], relay_send.at[i], unit_recv.at[u], at(4))
+            return remote(relay_buf.at[i], halo.at[3 * i + 1], relay_send.at[i], unit_recv.at[3 * i + 1], at(4))
         if at_x == 1:
-            u = via_two[i]
-            return remote(relay_buf.at[i], halo.at[u], relay_send.at[i], unit_recv.at[u], at(-1))
+            return remote(relay_buf.at[i], halo.at[3 * i], relay_send.at[i], unit_recv.at[3 * i], at(-1))
         return remote(relay_buf.at[i], relay_buf.at[i], relay_send.at[i], relay_recv.at[i], at(3))
 
     def relay_count(at_x):
@@ -223,13 +242,11 @@
 
     def relay(i, places):
         for at_x in places:
-            if i < relay_count(at_x):
-
-                @pl.when(x == at_x)
-                def _(at_x=at_x):
-                    copy = remote(relay_buf.at[i], relay_buf.at[i], relay_send.at[i], relay_recv.at[i], at(3))
-                    copy.wait_recv()
-                    relay_copy(i, at_x).start()
+
+            @pl.when((x == at_x) & (i < relay_count(at_x)))
+            def _(at_x=at_x):
+                remote(relay_buf.at[i], relay_buf.at[i], relay_send.at[i], relay_recv.at[i], at(3)).wait_recv()
+                relay_copy(i, at_x).start()
 
     for d in range(1, group):
         other = lax.rem(me + group - d, group)
@@ -246,6 +263,11 @@
     def _():
         inv_copy(1).start()
 
+    @pl.when(x == 3)
+    def _():
+        for c in range(early, chunks):
+            far_copy(c).start()
+
     def to_columns(row):
         return jnp.transpose(jnp.broadcast_to(row, (HEAD_DIM, row.shape[1])))
 
@@ -253,18 +275,16 @@
         return (values.astype(F32) * column * gain).astype(BF16)
 
     def gain_row(ref, h):
-        return ref[h]
+        return ref[pl.ds(pl.multiple_of(h * HEAD_DIM, HEAD_DIM), HEAD_DIM)].reshape(1, HEAD_DIM)
 
     col_own[...] = to_columns(inv_own[...])
 
     def norm_own(h, carry):
-        ql[h] = normed(ql[h], col_own[:rows], gain_row(qg_ref, h))
-        kl[h] = normed(kl[h], col_own[rows:], gain_row(kg_ref, h))
+        qn[h] = normed(ql[h], col_own[:rows], gain_row(qg_ref, h))
+        kn[h] = normed(kl[h], col_own[rows:], gain_row(kg_ref, h))
         return carry
 
     lax.fori_loop(0, heads, norm_own, 0)
-    for copy in loads(2):
-        copy.wait()
 
     def seen(h, t, back):
         target = t - back
@@ -299,14 +319,14 @@
         return peak, total, mixed
 
     def local(h, carry):
-        keys, values = kl[h], vl[h]
-        scores = dot_nt(keys[:tile], ql[h, :tile])
+        keys, values = kn[h], vl[h]
+        scores = dot_nt(keys[:tile], qn[h, :tile])
         peak = jnp.max(scores, axis=0, keepdims=True)
         probs = exps(scores, peak)
         ml[h, 0:1] = peak
         ml[h, 1:2] = row_sum(probs)
         acc[h, 0] = dot_tn(values[:tile], probs.astype(BF16))
-        peak, total, mixed = two_blocks(keys, values, ql[h, tile:], seen(h, first + 1, 1), None)
+        peak, total, mixed = two_blocks(keys, values, qn[h, tile:], seen(h, first + 1, 1), None)
         ml[h, 2:3] = peak
         ml[h, 3:4] = total
         acc[h, 1] = mixed
@@ -322,7 +342,7 @@
         q_copy(h).wait_recv()
         queries = normed(q_next[h], col_next[...], gain_row(qg_ref, h))
         peak, total, mixed = two_blocks(
-            kl[h], vl[h], queries, seen(h, first + 2, 2), seen(h, first + 2, 1)
+            kn[h], vl[h], queries, seen(h, first + 2, 2), seen(h, first + 2, 1)
         )
         ml_send[h, 0:1] = peak
         ml_send[h, 1:2] = total
@@ -330,15 +350,29 @@
         o_copy(h).start()
         return carry
 
-    relay(0, (0, 2))
-    lax.fori_loop(0, heads, local, 0)
-    relay(1, (0, 2))
+    def local_step(h, carry):
+        relay(h, (0, 2))
+
+        @pl.when((x < 3) & (h + near_early < heads))
+        def _():
+            for copy in near_copies(h + near_early):
+                copy.start()
+
+        return local(h, carry)
+
+    lax.fori_loop(0, heads, local_step, 0)
 
     @pl.when(x < 3)
     def _():
         inv_copy(1).wait_recv()
         col_next[...] = to_columns(inv_next[:, :tile])
-        lax.fori_loop(0, heads, for_next, 0)
+
+        def next_step(h, carry):
+            relay(h, (1,))
+            relay(heads + h, (0, 2))
+            return for_next(h, carry)
+
+        lax.fori_loop(0, heads, next_step, 0)
         ml_copy().start()
 
     inv_copy(0).wait_recv()
@@ -352,14 +386,19 @@
             out_buf.at[h], out_hbm.at[:, pl.ds(pl.multiple_of(h * HEAD_DIM, HEAD_DIM), HEAD_DIM)], out_sem.at[h]
         )
 
-    def unit_wait(u):
-        remote(halo.at[u], halo.at[u], unit_send.at[u], unit_recv.at[u], at(1)).wait_recv()
+    def part_wait(h, part):
+        for sub in range(SUB):
+            c = (4 * h + part) * SUB + sub
+            remote(halo.at[c], halo.at[c], unit_send.at[c], unit_recv.at[c], at(1)).wait_recv()
+
+    def arrived(h, part):
+        return halo[pl.ds((4 * h + part) * SUB, SUB)].reshape(tile, HEAD_DIM)
 
     def high_tile(h):
-        keys = normed(halo[4 * h], col_prev[tile:], gain_row(kg_ref, h))
-        values = halo[4 * h + 1]
+        keys = normed(arrived(h, 0), col_prev[tile:], gain_row(kg_ref, h))
+        values = arrived(h, 1)
         flag = seen(h, first + 1, 2)
-        scores = dot_nt(keys, ql[h, tile:])
+        scores = dot_nt(keys, qn[h, tile:])
         before = ml[h, 2:3]
         peak = jnp.maximum(before, top(scores, flag))
         probs = exps(scores, shift(peak, flag))
@@ -371,13 +410,13 @@
 
     def far_head(h):
         for part in range(4):
-            unit_wait(4 * h + part)
+            part_wait(h, part)
         keys_hi = high_tile(h)
-        keys_lo = normed(halo[4 * h + 2], col_prev[:tile], gain_row(kg_ref, h))
+        keys_lo = normed(arrived(h, 2), col_prev[:tile], gain_row(kg_ref, h))
         keys = jnp.concatenate([keys_lo, keys_hi], axis=0)
-        values = jnp.concatenate([halo[4 * h + 3], halo[4 * h + 1]], axis=0)
+        values = jnp.concatenate([arrived(h, 3), arrived(h, 1)], axis=0)
         peak_far, total_far, mixed_far = two_blocks(
-            keys, values, ql[h, :tile], seen(h, first, 2), seen(h, first, 1)
+            keys, values, qn[h, :tile], seen(h, first, 2), seen(h, first, 1)
         )
         merge(h, peak_far, total_far, mixed_far)
 
@@ -389,8 +428,8 @@
         out_copy(h).start()
 
     def near_high(h, carry):
-        unit_wait(4 * h)
-        unit_wait(4 * h + 1)
+        part_wait(h, 0)
+        part_wait(h, 1)
         high_tile(h)
         return carry
 
@@ -402,32 +441,27 @@
     def loop(lo, hi, body):
         lax.fori_loop(lo, hi, lambda h, c: body(h, c), 0)
 
+    def relays(lo, hi, at_x):
+        loop(lo, hi, lambda i, c: (relay(i, (at_x,)), c)[1])
+
     @pl.when(x == 0)
     def _():
-        done = 2
-        for h in range(heads):
-            need = (4 * h + 2) // 3 + 2
-            while done < min(need, len(via_zero)):
-                relay(done, (0,))
-                done += 1
-            far_head(h)
-        while done < len(via_zero):
-            relay(done, (0,))
-            done += 1
-
-    for at_x, start in ((1, 0), (2, 2)):
-
-        @pl.when(x == at_x)
-        def _(at_x=at_x, start=start):
-            left = list(range(start, len(via_two)))
-            split = max(0, len(left) - heads)
-            for i in left[:split]:
-                relay(i, (at_x,))
-            left = left[split:]
-            for h in range(heads):
-                if h < len(left):
-                    relay(left[h], (at_x,))
-                near_high(h, 0)
+        relays(2 * heads, len(via_zero), 0)
+        loop(0, heads, lambda h, c: (far_head(h), c)[1])
+
+    @pl.when(x == 1)
+    def _():
+        def step(h, carry):
+            relay(heads + h, (1,))
+            return near_high(h, carry)
+
+        loop(0, heads, step)
+        relays(2 * heads, len(via_two), 1)
+
+    @pl.when(x == 2)
+    def _():
+        relays(2 * heads, len(via_two), 2)
+        loop(0, heads, near_high)
 
     @pl.when(x == 3)
     def _():
@@ -452,14 +486,14 @@
 
     @pl.when(x == 3)
     def _():
-        for u in range(units):
-            far_copy(u).wait_send()
+        for c in range(chunks):
+            far_copy(c).wait_send()
 
     @pl.when(x < 3)
     def _():
-        for u in near_units:
-            near_copy(u).wait_send()
         for h in range(heads):
+            for copy in near_copies(h):
+                copy.wait_send()
             o_copy(h).wait_send()
         ml_copy().wait_send()
 
@@ -475,7 +509,7 @@
     seqs, group = lax.axis_size("seq"), lax.axis_size("head")
     rows, cols = q_proj.shape
     heads, tile = cols // HEAD_DIM, rows // 2
-    units = 4 * heads
+    chunks = 4 * heads * SUB
     via_two, via_zero, _ = routes(heads)
     slots = max(len(via_two), len(via_zero))
     dma = pltpu.SemaphoreType.DMA
@@ -492,8 +526,10 @@
             pltpu.VMEM((heads, rows, HEAD_DIM), BF16),
             pltpu.VMEM((heads, rows, HEAD_DIM), BF16),
             pltpu.VMEM((heads, rows, HEAD_DIM), BF16),
-            pltpu.VMEM((units, tile, HEAD_DIM), BF16),
-            pltpu.VMEM((slots, tile, HEAD_DIM), BF16),
+            pltpu.VMEM((heads, rows, HEAD_DIM), BF16),
+            pltpu.VMEM((heads, rows, HEAD_DIM), BF16),
+            pltpu.VMEM((chunks, tile // SUB, HEAD_DIM), BF16),
+            pltpu.VMEM((slots, tile // SUB, HEAD_DIM), BF16),
             pltpu.VMEM((heads, tile, HEAD_DIM), BF16),
             pltpu.VMEM((heads, HEAD_DIM, tile), BF16),
             pltpu.VMEM((heads, HEAD_DIM, tile), BF16),
@@ -510,8 +546,8 @@
             pltpu.VMEM((1, 2 * rows), F32),
             pltpu.VMEM((heads, rows, HEAD_DIM), BF16),
             dma((3, heads)),
-            dma((units,)),
-            dma((units,)),
+            dma((chunks,)),
+            dma((chunks,)),
             dma((slots,)),
             dma((slots,)),
             dma((heads,)),
@@ -525,7 +561,7 @@
             dma((heads,)),
         ],
         compiler_params=pltpu.CompilerParams(
-            collective_id=0, has_side_effects=True, vmem_limit_bytes=48 * 1024 * 1024
+            collective_id=0, has_side_effects=True, vmem_limit_bytes=62 * 1024 * 1024
         ),
         cost_estimate=pl.CostEstimate(flops=flops, bytes_accessed=4 * rows * cols * 2, transcendentals=0),
         name="window_attention",
@@ -533,8 +569,8 @@
         q_proj,
         k_proj,
         v_proj,
-        q_gain.reshape(heads, 1, HEAD_DIM),
-        k_gain.reshape(heads, 1, HEAD_DIM),
+        q_gain,
+        k_gain,
         window_tiles.transpose(0, 2, 1),
         window_count,
     )

time: 94.2 us -> 64.7 us (0.69)
  the two profiles are of different devices: /device:TPU:48 before, /device:TPU:128 now
where the time goes in v2:
time: 64.7 us; the launch traced here: 64.4 us
  Pallas kernels  62.2 us (96%)
  local copies, waits for them, and re-layouts  2.23 us (3%)
    pallas_call x1, Pallas kernels, per_device(): pl.pallas_call(functools.partial(kernel, seqs, group), out_shape=jax.Shap...  62.2 us
    unnamed x1, local copies, waits for them, and re-layouts  2.23 us

profile of v2, /device:TPU:128, one launch (start us, length us, event | category | flops | bytes accessed | tf_op | source)
XLA Modules:
  0.0 64.4 jit_solution(11124536369978296121)
XLA Ops:
  0.0 62.2 %window_attention.1 = bf16[768,640]{1,0:T(8,128)(2,1)} custom-call(bf16[768,640]{1,0:T(8,128)(2,1)} %q_hbm.1, bf16[768,640]{1,0:T(8,128)(2,1)} %k_hbm.1, bf16[768,640]{1,0:T(8,128)(2,1)} %v_hbm.1, f32[640]{0:T(1024)} %qg_ref.1, f32[640]{0:T(1024)} %kg_ref.1, s32[5,3,128]{2,1,0:T(4,128)} %bitcast.1, s32[5,128]{1,0:T(8,128)} %count_ref.1), custom_call_target="tpu_custom_call" | custom-call | flops 2831155200 | bytes 3932160 | tf_op jit(solution)/shard_map/window_attention/pallas_call | solution.py:520
  62.2 2.2 %copy.9 = bf16[768,640]{1,0:T(8,128)(2,1)} copy(bf16[768,640]{1,0:T(8,128)(2,1)} %window_attention.1) | data formatting | bytes 1966080

commit v3 on v2

--- a/solution.py
+++ b/solution.py
@@ -29,16 +29,31 @@
 
 SUB = 2
 FAR_EARLY = 3
+FAR_AHEAD = 1
+PER_DIRECT = 8
+Q_EVERY = 7
 NEAR_EARLY = 2
+
+
+def two_slot(i):
+    return 10 * (i // 2) + 6 * (i % 2)
+
+
+def one_slot(i):
+    return two_slot(i) + 1
+
+
+def zero_slot(i):
+    return 10 * (i // 3) + 3 * (i % 3) + 2
 
 
 def routes(heads):
     chunks = 4 * heads * SUB
-    two, zero = (chunks * 3) // 10, (chunks * 13) // 40
-    via_two = [3 * i for i in range(two)]
-    via_zero = [3 * i + 1 for i in range(zero)]
-    direct = [c for c in range(chunks) if c not in via_two and c not in via_zero]
-    return via_two, via_zero, direct
+    via_two, via_one, via_zero = (
+        [slot(i) for i in range(chunks) if slot(i) < chunks] for slot in (two_slot, one_slot, zero_slot)
+    )
+    direct = [c for c in range(chunks) if c not in via_two + via_one + via_zero]
+    return via_two, via_one, via_zero, direct
 
 
 def kernel(
@@ -47,11 +62,15 @@
     q_hbm,
     k_hbm,
     v_hbm,
+    qg_in,
+    kg_in,
+    tiles_in,
+    count_in,
+    out_hbm,
     qg_ref,
     kg_ref,
     tiles_ref,
     count_ref,
-    out_hbm,
     ql,
     kl,
     vl,
@@ -59,6 +78,7 @@
     kn,
     halo,
     relay_buf,
+    relay_b,
     q_next,
     o_send,
     o_recv,
@@ -75,10 +95,13 @@
     inv_next,
     out_buf,
     load_sem,
+    small_sem,
     unit_send,
     unit_recv,
     relay_send,
     relay_recv,
+    relay_b_send,
+    relay_b_recv,
     q_send_sem,
     q_recv_sem,
     o_send_sem,
@@ -94,7 +117,7 @@
     model = heads * HEAD_DIM * group
     piece = tile // SUB
     chunks = 4 * heads * SUB
-    via_two, via_zero, direct = routes(heads)
+    via_two, via_one, via_zero, direct = routes(heads)
     s = lax.axis_index("seq")
     me = lax.axis_index("head")
     x = lax.rem(s, 4)
@@ -107,6 +130,35 @@
         return pltpu.make_async_remote_copy(
             src_ref=src, dst_ref=dst, send_sem=send, recv_sem=recv, device_id=where, device_id_type=MESH
         )
+
+    barrier = pltpu.get_barrier_semaphore()
+
+    def greet(where):
+        pl.semaphore_signal(barrier, inc=1, device_id=where, device_id_type=MESH)
+
+    greet(at(1))
+    greet(at(-1))
+
+    @pl.when((x == 0) | (x == 2))
+    def _():
+        greet(at(3))
+
+    @pl.when((x == 1) | (x == 3))
+    def _():
+        greet(at(-3))
+
+    @pl.when(x == 0)
+    def _():
+        greet(at(4))
+        greet(at(-4))
+        greet(at(-3))
+
+    @pl.when(x == 1)
+    def _():
+        greet(at(3))
+
+    for d in range(1, group):
+        greet({"seq": s, "head": lax.rem(me + d, group)})
 
     def loads(which):
         src, dst = ((q_hbm, ql), (k_hbm, kl), (v_hbm, vl))[which]
@@ -115,33 +167,17 @@
             for h in range(heads)
         ]
 
+    small = [
+        pltpu.make_async_copy(src, dst, small_sem.at[n])
+        for n, (src, dst) in enumerate(
+            ((qg_in, qg_ref), (kg_in, kg_ref), (tiles_in, tiles_ref), (count_in, count_ref))
+        )
+    ]
     for which in range(3):
         for copy in loads(which):
             copy.start()
-
-    barrier = pltpu.get_barrier_semaphore()
-
-    def greet(where):
-        pl.semaphore_signal(barrier, inc=1, device_id=where, device_id_type=MESH)
-
-    greet(at(1))
-    greet(at(-1))
-
-    @pl.when((x == 0) | (x == 2))
-    def _():
-        greet(at(3))
-
-    @pl.when((x == 1) | (x == 3))
-    def _():
-        greet(at(-3))
-
-    @pl.when(x == 0)
-    def _():
-        greet(at(4))
-        greet(at(-4))
-
-    for d in range(1, group):
-        greet({"seq": s, "head": lax.rem(me + d, group)})
+    for copy in small:
+        copy.start()
 
     ones = jnp.ones((8, HEAD_DIM), BF16)
     for which, buf in ((0, ql), (1, kl)):
@@ -150,22 +186,28 @@
 
         def square_sum(h, total, buf=buf):
             wide = buf[h].astype(F32)
-            sq = wide * wide
-            hi = sq.astype(BF16)
-            lo = (sq - hi.astype(F32)).astype(BF16)
-            return total + dot_nt(ones, hi) + dot_nt(ones, lo)
-
-        total = lax.fori_loop(0, heads, square_sum, jnp.zeros((8, rows), F32))
+            return total + wide * wide
+
+        left = lax.fori_loop(1, heads, square_sum, square_sum(0, 0.0))
+        total = jnp.zeros((8, rows), F32)
+        for _ in range(3):
+            term = left.astype(BF16)
+            total = total + dot_nt(ones, term)
+            left = left - term.astype(F32)
         stats[me, :, which * rows : (which + 1) * rows] = total[:1]
 
-    for copy in loads(2):
+    for copy in loads(2) + small:
         copy.wait()
 
     @pl.when(x == 0)
     def _():
-        pl.semaphore_wait(barrier, group - 1 + 5)
-
-    @pl.when(x > 0)
+        pl.semaphore_wait(barrier, group - 1 + 6)
+
+    @pl.when(x == 1)
+    def _():
+        pl.semaphore_wait(barrier, group - 1 + 4)
+
+    @pl.when(x > 1)
     def _():
         pl.semaphore_wait(barrier, group - 1 + 3)
 
@@ -199,6 +241,9 @@
         if c in via_two:
             i = via_two.index(c)
             return remote(chunk_src(c), relay_buf.at[i], unit_send.at[c], relay_recv.at[i], at(-1))
+        if c in via_one:
+            i = via_one.index(c)
+            return remote(chunk_src(c), relay_b.at[i], unit_send.at[c], relay_b_recv.at[i], at(-1))
         if c in via_zero:
             i = via_zero.index(c)
             return remote(chunk_src(c), relay_buf.at[i], unit_send.at[c], relay_recv.at[i], at(-3))
@@ -207,34 +252,42 @@
     def q_copy(h):
         return remote(ql.at[h, pl.ds(0, tile)], q_next.at[h], q_send_sem.at[h], q_recv_sem.at[h], at(-1))
 
-    early = min(FAR_EARLY, chunks)
+    early = sorted(via_one[:FAR_EARLY] + via_two[:FAR_EARLY] + via_zero[:FAR_EARLY])
+    relayed = [c for c in sorted(via_one + via_two + via_zero) if c not in early]
+    late, waiting = [], list(direct)
+    while relayed or waiting:
+        late, waiting = late + waiting[:1], waiting[1:]
+        late, relayed = late + relayed[:PER_DIRECT], relayed[PER_DIRECT:]
     near_early = min(NEAR_EARLY, heads)
 
     @pl.when(x == 3)
     def _():
-        for c in range(early):
+        for c in early:
             far_copy(c).start()
-            if c % 2 == 1 and c // 2 < heads:
-                q_copy(c // 2).start()
-        for h in range(early // 2, heads):
-            q_copy(h).start()
-
-    @pl.when((x > 0) & (x < 3))
-    def _():
-        for h in range(heads):
-            q_copy(h).start()
-
-    @pl.when(x < 3)
-    def _():
-        for h in range(near_early):
-            for copy in near_copies(h):
-                copy.start()
+        q_copy(0).start()
+
+    def near_start(h):
+        for half in range(2):
+
+            @pl.when(x < 3)
+            def _(half=half):
+                for copy in near_copies(h)[half * SUB : (half + 1) * SUB]:
+                    copy.start()
+
+            if half == 0:
+
+                @pl.when((x > 0) & (x < 3))
+                def _():
+                    q_copy(h).start()
+
+    for h in range(near_early):
+        near_start(h)
 
     def relay_copy(i, at_x):
         if at_x == 0:
-            return remote(relay_buf.at[i], halo.at[3 * i + 1], relay_send.at[i], unit_recv.at[3 * i + 1], at(4))
+            return remote(relay_buf.at[i], halo.at[zero_slot(i)], relay_send.at[i], unit_recv.at[zero_slot(i)], at(4))
         if at_x == 1:
-            return remote(relay_buf.at[i], halo.at[3 * i], relay_send.at[i], unit_recv.at[3 * i], at(-1))
+            return remote(relay_buf.at[i], halo.at[two_slot(i)], relay_send.at[i], unit_recv.at[two_slot(i)], at(-1))
         return remote(relay_buf.at[i], relay_buf.at[i], relay_send.at[i], relay_recv.at[i], at(3))
 
     def relay_count(at_x):
@@ -248,6 +301,18 @@
                 remote(relay_buf.at[i], relay_buf.at[i], relay_send.at[i], relay_recv.at[i], at(3)).wait_recv()
                 relay_copy(i, at_x).start()
 
+    def relay_b_copy(i, at_x):
+        if at_x == 1:
+            c = one_slot(i)
+            return remote(relay_b.at[i], halo.at[c], relay_b_send.at[i], unit_recv.at[c], at(3))
+        return remote(relay_b.at[i], relay_b.at[i], relay_b_send.at[i], relay_b_recv.at[i], at(-1))
+
+    def relay_one(i, at_x):
+        @pl.when((x == at_x) & (i < len(via_one)))
+        def _():
+            remote(relay_b.at[i], relay_b.at[i], relay_b_send.at[i], relay_b_recv.at[i], at(-1)).wait_recv()
+            relay_b_copy(i, at_x).start()
+
     for d in range(1, group):
         other = lax.rem(me + group - d, group)
         remote(stats.at[other], stats.at[other], stat_send.at[d], stat_recv.at[other], at(1)).wait_recv()
@@ -265,8 +330,12 @@
 
     @pl.when(x == 3)
     def _():
-        for c in range(early, chunks):
+        for n, c in enumerate(late):
             far_copy(c).start()
+            if n % Q_EVERY == 1 and n // Q_EVERY + 1 < heads:
+                q_copy(n // Q_EVERY + 1).start()
+        for h in range((len(late) - 2) // Q_EVERY + 2, heads):
+            q_copy(h).start()
 
     def to_columns(row):
         return jnp.transpose(jnp.broadcast_to(row, (HEAD_DIM, row.shape[1])))
@@ -351,12 +420,12 @@
         return carry
 
     def local_step(h, carry):
+        relay_one(h, 2)
         relay(h, (0, 2))
 
-        @pl.when((x < 3) & (h + near_early < heads))
+        @pl.when(h + near_early < heads)
         def _():
-            for copy in near_copies(h + near_early):
-                copy.start()
+            near_start(h + near_early)
 
         return local(h, carry)
 
@@ -368,8 +437,10 @@
         col_next[...] = to_columns(inv_next[:, :tile])
 
         def next_step(h, carry):
+            relay_one(heads + h, 2)
+            relay(heads + h, (0, 2))
+            relay_one(h, 1)
             relay(h, (1,))
-            relay(heads + h, (0, 2))
             return for_next(h, carry)
 
         lax.fori_loop(0, heads, next_step, 0)
@@ -446,12 +517,21 @@
 
     @pl.when(x == 0)
     def _():
-        relays(2 * heads, len(via_zero), 0)
-        loop(0, heads, lambda h, c: (far_head(h), c)[1])
+        tail = len(via_zero) - 2 * heads
+
+        relays(2 * heads, 2 * heads + tail - FAR_AHEAD, 0)
+
+        def step(h, carry):
+            relay(2 * heads + tail - FAR_AHEAD + h, (0,))
+            far_head(h)
+            return carry
+
+        loop(0, heads, step)
 
     @pl.when(x == 1)
     def _():
         def step(h, carry):
+            relay_one(heads + h, 1)
             relay(heads + h, (1,))
             return near_high(h, carry)
 
@@ -503,6 +583,9 @@
         def _(at_x=at_x):
             for i in range(relay_count(at_x)):
                 relay_copy(i, at_x).wait_send()
+            if at_x > 0:
+                for i in range(len(via_one)):
+                    relay_b_copy(i, at_x).wait_send()
 
 
 def per_device(q_proj, k_proj, v_proj, q_gain, k_gain, window_tiles, window_count):
@@ -510,19 +593,23 @@
     rows, cols = q_proj.shape
     heads, tile = cols // HEAD_DIM, rows // 2
     chunks = 4 * heads * SUB
-    via_two, via_zero, _ = routes(heads)
+    via_two, via_one, via_zero, _ = routes(heads)
     slots = max(len(via_two), len(via_zero))
+    slots_b = len(via_one)
     dma = pltpu.SemaphoreType.DMA
     anywhere = pl.BlockSpec(memory_space=pl.ANY)
-    vmem = pl.BlockSpec(memory_space=pltpu.VMEM)
-    smem = pl.BlockSpec(memory_space=pltpu.SMEM)
+    hbm = pl.BlockSpec(memory_space=pltpu.HBM)
     flops = 30 * heads * tile * tile * HEAD_DIM
     return pl.pallas_call(
         functools.partial(kernel, seqs, group),
         out_shape=jax.ShapeDtypeStruct((rows, cols), BF16),
-        in_specs=[anywhere] * 3 + [vmem] * 2 + [smem] * 2,
+        in_specs=[hbm] * 7,
         out_specs=anywhere,
         scratch_shapes=[
+            pltpu.VMEM(q_gain.shape, F32),
+            pltpu.VMEM(k_gain.shape, F32),
+            pltpu.SMEM((heads, WIN, window_count.shape[1]), jnp.int32),
+            pltpu.SMEM(window_count.shape, jnp.int32),
             pltpu.VMEM((heads, rows, HEAD_DIM), BF16),
             pltpu.VMEM((heads, rows, HEAD_DIM), BF16),
             pltpu.VMEM((heads, rows, HEAD_DIM), BF16),
@@ -530,6 +617,7 @@
             pltpu.VMEM((heads, rows, HEAD_DIM), BF16),
             pltpu.VMEM((chunks, tile // SUB, HEAD_DIM), BF16),
             pltpu.VMEM((slots, tile // SUB, HEAD_DIM), BF16),
+            pltpu.VMEM((slots_b, tile // SUB, HEAD_DIM), BF16),
             pltpu.VMEM((heads, tile, HEAD_DIM), BF16),
             pltpu.VMEM((heads, HEAD_DIM, tile), BF16),
             pltpu.VMEM((heads, HEAD_DIM, tile), BF16),
@@ -546,10 +634,13 @@
             pltpu.VMEM((1, 2 * rows), F32),
             pltpu.VMEM((heads, rows, HEAD_DIM), BF16),
             dma((3, heads)),
+            dma((4,)),
             dma((chunks,)),
             dma((chunks,)),
             dma((slots,)),
             dma((slots,)),
+            dma((slots_b,)),
+            dma((slots_b,)),
             dma((heads,)),
             dma((heads,)),
             dma((heads,)),

time: 64.7 us -> 56.7 us (0.88)
  the two profiles are of different devices: /device:TPU:128 before, /device:TPU:1 now
where the time goes in v3:
time: 56.7 us; the launch traced here: 56.5 us
  Pallas kernels  54.3 us (96%)
  local copies, waits for them, and re-layouts  2.23 us (4%)
    pallas_call x1, Pallas kernels, per_device(): pl.pallas_call(functools.partial(kernel, seqs, group), out_shape=jax.Shap...  54.3 us
    unnamed x1, local copies, waits for them, and re-layouts  2.23 us

profile of v3, /device:TPU:1, one launch (start us, length us, event | category | flops | bytes accessed | tf_op | source)
XLA Modules:
  0.0 56.5 jit_solution(10747841310210728351)
XLA Ops:
  0.0 54.3 %window_attention.1 = bf16[768,640]{1,0:T(8,128)(2,1)} custom-call(bf16[768,640]{1,0:T(8,128)(2,1)} %q_hbm.1, bf16[768,640]{1,0:T(8,128)(2,1)} %k_hbm.1, bf16[768,640]{1,0:T(8,128)(2,1)} %v_hbm.1, f32[640]{0:T(1024)} %qg_in.1, f32[640]{0:T(1024)} %kg_in.1, s32[5,3,128]{2,1,0:T(4,128)} %bitcast.1, s32[5,128]{1,0:T(8,128)} %count_in.1), custom_call_target="tpu_custom_call" | custom-call | flops 2831155200 | bytes 3932160 | tf_op jit(solution)/shard_map/window_attention/pallas_call | solution.py:603
  54.3 2.2 %copy.9 = bf16[768,640]{1,0:T(8,128)(2,1)} copy(bf16[768,640]{1,0:T(8,128)(2,1)} %window_attention.1) | data formatting | bytes 1966080

commit v4 on v3

--- a/solution.py
+++ b/solution.py
@@ -652,18 +652,15 @@
             dma((heads,)),
         ],
         compiler_params=pltpu.CompilerParams(
-            collective_id=0, has_side_effects=True, vmem_limit_bytes=62 * 1024 * 1024
+            collective_id=0, has_side_effects=True, vmem_limit_bytes=48 * 1024 * 1024
         ),
         cost_estimate=pl.CostEstimate(flops=flops, bytes_accessed=4 * rows * cols * 2, transcendentals=0),
         name="window_attention",
     )(
-        q_proj,
-        k_proj,
-        v_proj,
-        q_gain,
-        k_gain,
-        window_tiles.transpose(0, 2, 1),
-        window_count,
+        *(
+            pltpu.with_memory_space_constraint(a, pltpu.HBM)
+            for a in (q_proj, k_proj, v_proj, q_gain, k_gain, window_tiles.transpose(0, 2, 1), window_count)
+        )
     )
 
 

time: 56.7 us -> 54.8 us (0.966)
  local copies, waits for them, and re-layouts: 2.23 us -> 0.95 us
  Pallas kernels: 54.3 us -> 53.7 us
    unnamed x1, local copies, waits for them, and re-layouts: 2.23 us -> 0.95 us
    pallas_call x1, Pallas kernels: 54.3 us -> 53.7 us  [per_device(): pl.pallas_call(functools.partial(kernel, seqs, group), out_shape=jax.Shap...]
where the time goes in v4:
time: 54.8 us; the launch traced here: 54.6 us
  Pallas kernels  53.7 us (98%)
  local copies, waits for them, and re-layouts  0.95 us (2%)
    pallas_call x1, Pallas kernels, per_device(): pl.pallas_call(functools.partial(kernel, seqs, group), out_shape=jax.Shap...  53.7 us

profile of v4, /device:TPU:1, one launch (start us, length us, event | category | flops | bytes accessed | tf_op | source)
XLA Modules:
  0.0 54.6 jit_solution(1383352534049703412)
XLA Ops:
  0.0 53.7 %window_attention.1 = bf16[768,640]{1,0:T(8,128)(2,1)S(1)} custom-call(bf16[768,640]{1,0:T(8,128)(2,1)} %q_hbm.1, bf16[768,640]{1,0:T(8,128)(2,1)} %k_hbm.1, bf16[768,640]{1,0:T(8,128)(2,1)} %v_hbm.1, f32[640]{0:T(1024)} %qg_in.1, f32[640]{0:T(1024)} %kg_in.1, s32[5,3,128]{2,1,0:T(4,128)} %bitcast.1, s32[5,128]{1,0:T(8,128)} %count_in.1), custom_call_target="tpu_custom_call" | custom-call | flops 2831155200 | bytes 3932160 | tf_op jit(solution)/shard_map/window_attention/pallas_call | solution.py:603
  53.7 0.9 %copy.9 = bf16[768,640]{1,0:T(8,128)(2,1)} copy(bf16[768,640]{1,0:T(8,128)(2,1)S(1)} %window_attention.1) | data formatting | bytes 1966080

commit v5 on v4

--- a/solution.py
+++ b/solution.py
@@ -28,9 +28,9 @@
 
 
 SUB = 2
-FAR_EARLY = 3
+FAR_EARLY = 4
 FAR_AHEAD = 1
-PER_DIRECT = 8
+PER_DIRECT = 10
 Q_EVERY = 7
 NEAR_EARLY = 2
 

time: 54.8 us -> 54.9 us (level)
  no operation moved by 1% of the time
where the time goes in v5:
time: 54.9 us; the launch traced here: 54.8 us
  Pallas kernels  53.8 us (98%)
  local copies, waits for them, and re-layouts  0.95 us (2%)
    pallas_call x1, Pallas kernels, per_device(): pl.pallas_call(functools.partial(kernel, seqs, group), out_shape=jax.Shap...  53.8 us

profile of v5, /device:TPU:1, one launch (start us, length us, event | category | flops | bytes accessed | tf_op | source)
XLA Modules:
  0.0 54.8 jit_solution(10507412738683259239)
XLA Ops:
  0.0 53.8 %window_attention.1 = bf16[768,640]{1,0:T(8,128)(2,1)S(1)} custom-call(bf16[768,640]{1,0:T(8,128)(2,1)} %q_hbm.1, bf16[768,640]{1,0:T(8,128)(2,1)} %k_hbm.1, bf16[768,640]{1,0:T(8,128)(2,1)} %v_hbm.1, f32[640]{0:T(1024)} %qg_in.1, f32[640]{0:T(1024)} %kg_in.1, s32[5,3,128]{2,1,0:T(4,128)} %bitcast.1, s32[5,128]{1,0:T(8,128)} %count_in.1), custom_call_target="tpu_custom_call" | custom-call | flops 2831155200 | bytes 3932160 | tf_op jit(solution)/shard_map/window_attention/pallas_call | solution.py:603
  53.8 0.9 %copy.9 = bf16[768,640]{1,0:T(8,128)(2,1)} copy(bf16[768,640]{1,0:T(8,128)(2,1)S(1)} %window_attention.1) | data formatting | bytes 1966080
